TPU v7x, 128 devices: a whole 4x4x4 slice. The times are simulated.
128 devices in a mesh: face: 8 (over y, core), elem: 16 (over z, x).
Axes of the slice: x: 4, y: 4, z: 4, core: 2. Of those that a mesh axis runs over, the one named last changes fastest.
Arguments:
- amount: float32 [24, 32768], P(None, ('face', 'elem')), may hold values from 0.05 to 1
- scatter: float32 [24, 32768], P(None, ('face', 'elem')), may hold values from 0.02 to 0.6
- cloud_path: float32 [24, 32768], P(None, ('face', 'elem')), may hold values from 0.01 to 1
- planck: float32 [24, 32768], P(None, ('face', 'elem')), may hold values from 0.4 to 1.6
- thickness: float32 [24, 32768], P(None, ('face', 'elem')), may hold values from 0.5 to 2
- corner_weights: float32 [8, 24, 32768], P(None, None, ('face', 'elem')), may hold values from 0 to 1, as said below
- table_index: int32 [24, 32768], P(None, ('face', 'elem')), may hold values from 0 to 6658, as said below
- cosine: float32 [32768], P(('face', 'elem')), may hold values from 0.1 to 1
- albedo: float32 [32768], P(('face', 'elem')), may hold values from 0.05 to 0.6
- surface_source: float32 [32768], P(('face', 'elem')), may hold values from 0.8 to 1.6
- stretch_map: int32 [32768], replicated, may hold values from 0 to 32767, as said below
- sunlit: int32 [256], P(('face', 'elem')), may hold values from 0 to 1, as said below
- table_longwave: bfloat16 [7560, 256], replicated, may hold values from 0.0099487305 to 2
- table_shortwave: bfloat16 [7560, 224], replicated, may hold values from 0.0049743652 to 1
- cloud_longwave: float32 [256], replicated, may hold values from 0.05 to 2
- cloud_shortwave: float32 [224], replicated, may hold values from 0.05 to 2
- planck_fraction: float32 [256], replicated, may hold values from 0.3 to 3
- rayleigh: float32 [224], replicated, may hold values from 0.05 to 1
- solar_flux: float32 [224], replicated, may hold values from 0.3 to 3
Outputs:
- heating_longwave: float32 [24, 32768], P(None, ('face', 'elem'))
- heating_shortwave: float32 [24, 32768], P(None, ('face', 'elem'))
Inputs may be any that keep to these rules, and one draw needn't show every extreme that they name: `stretch_map`: A permutation: each device's 256 dynamics columns hold exactly 2 positions in each device's range of 256 physics positions. Exactly 128 blocks are sunlit; in every draw some device has all its 2 blocks sunlit. table_index = e * 14 * 60 + t * 60 + p with e < 8, t < 13, p < 59. `corner_weights`: trilinear weights: corner 4 e + 2 t + p is the product of the three fractions or their complements; the eight of a level sum to one.
All inputs are finite; a program needn't handle non-finite values.
Results may differ from a plain program's by a relative error of at most 0.0011.
Values sent between devices are 32-bit elements; how exact they have to be, the bound alone decides.
A program may use at most 64 MiB of HBM per device.

v0:
```python
import functools
import math
import jax
import jax.numpy as jnp
from jax import lax
from jax.experimental import pallas as pl
from jax.experimental.pallas import tpu as pltpu
from jax.sharding import PartitionSpec as P

LEVELS = 24
NT_TEMP = 14
NT_PRES = 60
NTAB = 7560
COLS = 256
PEERS = 128
FULL = NTAB // 16 * 16
SCALE = -0.83 / math.log(2.0)
CORNERS = tuple(4 * (e * NT_TEMP * NT_PRES + t * NT_PRES) for e in range(2) for t in range(2))
GROUP = 32
WIDE = 16


def iota(shape, axis):
    return lax.broadcasted_iota(jnp.int32, shape, axis)


def parts(x):
    high = x.astype(jnp.bfloat16)
    rest = x - high.astype(jnp.float32)
    middle = rest.astype(jnp.bfloat16)
    low = (rest - middle.astype(jnp.float32)).astype(jnp.bfloat16)
    return (low, middle, high)


def pick(chooser, x, contract=0):
    total = None
    for part in parts(x):
        term = lax.dot_general(
            chooser, part, (((1,), (contract,)), ((), ())), preferred_element_type=jnp.float32
        )
        total = term if total is None else total + term
    return total


def as_row(pair):
    return jnp.concatenate([pair[0:1], pair[1:2]], axis=1)


def eye():
    return iota((COLS, COLS), 0) == iota((COLS, COLS), 1)


def to_column(row):
    return jnp.sum(jnp.where(eye(), row, 0.0), axis=1, keepdims=True)


def to_row(column):
    return jnp.sum(jnp.where(eye(), column, 0.0), axis=0, keepdims=True)


def onehot(mask):
    return jnp.where(mask, 1.0, 0.0).astype(jnp.bfloat16)


def slots_of(targets):
    target_row = as_row(targets)
    owner = (target_row >> 8).astype(jnp.float32)
    position = (target_row & 255).astype(jnp.float32)
    earlier = (to_column(owner) == owner) & (iota((COLS, COLS), 0) < iota((COLS, COLS), 1))
    rank = jnp.sum(jnp.where(earlier, 1.0, 0.0), axis=0, keepdims=True)
    return 2.0 * owner + rank, position


def fill_table(long_in, short_in, table):
    def long_rows(base, count):
        rows = long_in[pl.ds(base, count), :].astype(jnp.float32) * 2.0
        table[pl.ds(base * 4, count, 4), :] = rows[:, :128]
        table[pl.ds(base * 4 + 1, count, 4), :] = rows[:, 128:]

    def long_body(step, carry):
        for inner in range(8):
            long_rows(pl.multiple_of(step * 128, 128) + inner * 16, 16)
        return carry

    lax.fori_loop(0, FULL // 128, long_body, 0)
    long_rows(FULL, NTAB - FULL)

    def short_rows(block, base, count):
        unit = onehot(iota((count, count), 0) == iota((count, count), 1))
        rows = lax.dot_general(
            unit, block, (((1,), (1,)), ((), ())), preferred_element_type=jnp.float32
        )
        table[pl.ds(base * 4 + 2, count, 4), :] = rows[:, :128]
        table[pl.ds(base * 4 + 3, count, 4), :] = rows[:, 128:]

    def short_body(step, carry):
        base = pl.multiple_of(step * 256, 256)
        short_rows(short_in[:, pl.ds(base, 256)], base, 256)
        return carry

    short_in[224:256, :] = jnp.zeros((32, NTAB), jnp.bfloat16)
    lax.fori_loop(0, NTAB // 256, short_body, 0)
    short_rows(short_in[:, FULL - 128:FULL], FULL - 128, 128)
    short_rows(short_in[:, FULL:NTAB], FULL, NTAB - FULL)


def spread_weights(weights, lanes):
    source, lane = iota((64, 256), 0), iota((64, 256), 1)
    expand = onehot((source // 8 == (lane // 4) % 8) & (source % 8 == lane // 32))
    for third in range(3):
        low = weights[:, third * 8:third * 8 + 8, :].reshape(64, COLS).astype(jnp.bfloat16)
        lanes[third * COLS:(third + 1) * COLS, :] = lax.dot_general(
            low, expand, (((0,), (0,)), ((), ())), preferred_element_type=jnp.float32
        )


def gather(rows, table, lanes, kappa):
    out_row, lane = iota((32, 256), 0), iota((32, 256), 1)
    mask = (out_row // 4 == lane // 32) & (out_row % 4 == lane % 4)

    def body(step, carry):
        third = step // (COLS // GROUP)
        first = step % (COLS // GROUP) * GROUP
        for member in range(GROUP):
            place = step * GROUP + member
            picked = []
            for level in range(8):
                base = rows[third * 8 + level, first + member]
                for corner in CORNERS:
                    picked.append(table[pl.ds(base + corner, 8), :])
            right = jnp.concatenate(picked, axis=0).astype(jnp.bfloat16)
            weight = jnp.broadcast_to(lanes[pl.ds(place, 1), :], (32, 256))
            left = jnp.where(mask, weight, 0.0).astype(jnp.bfloat16)
            kappa[pl.ds(pl.multiple_of(place * 32, 32), 32), :] = jnp.dot(
                left, right, preferred_element_type=jnp.float32
            )
        return carry

    lax.fori_loop(0, 3 * COLS // GROUP, body, 0)


def radiate(state, kappa, heat, lit, params, held):
    cloud_long, planck_part, cloud_short, ray, flux = params
    lane = iota((WIDE, 128), 1)

    def body(step, carry):
        start = pl.multiple_of(step * WIDE, WIDE)
        fields = state[pl.ds(start, WIDE), :]
        scaled = fields * SCALE

        def wide(x, at):
            return jnp.broadcast_to(x[:, at:at + 1], (WIDE, 128))

        cosine = wide(fields, 120)
        albedo = wide(fields, 121)
        surface = wide(fields, 122)
        path = (1.0 / 0.83) / cosine
        down = [jnp.zeros((WIDE, 128), jnp.float32) for _ in range(2)]
        sdown = [jnp.zeros((WIDE, 128), jnp.float32) for _ in range(2)]
        direct = [jnp.ones((WIDE, 128), jnp.float32) for _ in range(2)]
        for level in range(LEVELS):
            amount = wide(scaled, 24 + level)
            scatter = wide(scaled, 48 + level)
            cloud = wide(scaled, 72 + level)
            planck = wide(fields, 96 + level)
            origin = (level // 8 * COLS + start) * 32 + level % 8 * 4
            for half in range(2):
                value = kappa[pl.ds(origin + half, WIDE, 32), :]
                absorb = 1.0 - jnp.exp2(amount * value + cloud * cloud_long[half])
                gain = absorb * (planck - down[half])
                down[half] = down[half] + gain
                held[level, half] = absorb
                held[level, 2 + half] = gain
            for half in range(2):
                value = kappa[pl.ds(origin + 2 + half, WIDE, 32), :]
                absorbed = amount * value
                scattered = scatter * ray[half] + cloud * cloud_short[half]
                extinct = absorbed + scattered
                lost = direct[half] * (1.0 - jnp.exp2(extinct * path))
                direct[half] = direct[half] - lost
                kept = lost * (absorbed / extinct)
                source = 0.5 * (lost - kept)
                close = 1.0 - jnp.exp2(extinct + absorbed)
                taken = close * sdown[half]
                sdown[half] = sdown[half] - taken + source
                held[level, 4 + half] = close
                held[level, 6 + half] = source
                held[level, 8 + half] = taken + kept
        up = [surface, surface]
        sup = [albedo * (direct[half] + sdown[half]) for half in range(2)]
        result = jnp.zeros((WIDE, 128), jnp.float32)
        for level in reversed(range(LEVELS)):
            planck = wide(fields, 96 + level)
            long_sum, short_sum = None, None
            for half in range(2):
                gain = held[level, half] * (planck - up[half])
                up[half] = up[half] + gain
                term = (gain + held[level, 2 + half]) * planck_part[half]
                long_sum = term if half == 0 else long_sum + term
                taken = held[level, 4 + half] * sup[half]
                sup[half] = sup[half] - taken + held[level, 6 + half]
                term = (taken + held[level, 8 + half]) * flux[half]
                short_sum = term if half == 0 else short_sum + term
            result = jnp.where(lane == level, jnp.sum(long_sum, axis=1, keepdims=True), result)
            result = jnp.where(
                lane == LEVELS + level, jnp.sum(short_sum, axis=1, keepdims=True), result
            )
        flag = jnp.where(step < PEERS // WIDE, lit[0], lit[1]).astype(jnp.float32)
        is_long = lane < LEVELS
        thickness = jnp.where(is_long, fields, pltpu.roll(fields, LEVELS, 1))
        factor = jnp.where(is_long, -1.0 / 256.0, cosine * (flag / 224.0))
        keep = lane < 2 * LEVELS
        heat[pl.ds(start, WIDE), :] = jnp.where(
            keep, result * factor / jnp.where(keep, thickness, 1.0), 0.0
        )
        return carry

    lax.fori_loop(0, COLS // WIDE, body, 0)


def two(row):
    return [jnp.broadcast_to(row[:, 0:128], (WIDE, 128)), jnp.broadcast_to(row[:, 128:256], (WIDE, 128))]


def short_row(ref, fill):
    row = ref[...]
    return jnp.concatenate([row, jnp.full((1, 32), fill, jnp.float32)], axis=1)


def exchange(count, me, outgoing, incoming, send_sem, recv_sem):
    def copy_to(step):
        peer = lax.rem(me + step, count)
        return pltpu.make_async_remote_copy(
            src_ref=outgoing.at[peer],
            dst_ref=incoming.at[me],
            send_sem=send_sem,
            recv_sem=recv_sem,
            device_id=(peer // 16, lax.rem(peer, 16)),
            device_id_type=pl.DeviceIdType.MESH,
        )

    def start(step, carry):
        copy_to(step).start()
        return carry

    lax.fori_loop(1, count, start, 0)


def await_all(count, outgoing, incoming, send_sem, recv_sem):
    most = count - 1
    pltpu.make_async_copy(
        outgoing.at[pl.ds(0, most)], incoming.at[pl.ds(0, most)], send_sem
    ).wait()
    pltpu.make_async_copy(
        outgoing.at[pl.ds(0, most)], incoming.at[pl.ds(0, most)], recv_sem
    ).wait()


def load_tables(long_hbm, short_hbm, long_in, short_in, sems):
    copies = []
    for piece in range(4):
        part = pl.ds(piece * 1920, min(1920, NTAB - piece * 1920))
        copies.append(
            pltpu.make_async_copy(long_hbm.at[part], long_in.at[part], sems.at[piece])
        )
    for piece in range(2):
        part = pl.ds(piece * 112, 112)
        copies.append(
            pltpu.make_async_copy(short_hbm.at[part], short_in.at[part], sems.at[4 + piece])
        )
    return copies


def column_kernel(
    lit,
    targets,
    amount,
    scatter,
    cloud_path,
    planck,
    thickness,
    cosine,
    albedo,
    surface,
    weights,
    index,
    cloud_long,
    cloud_short,
    planck_part,
    ray,
    flux,
    long_hbm,
    short_hbm,
    long_out,
    short_out,
    table,
    long_in,
    short_in,
    rows_v,
    rows,
    lanes,
    kappa,
    state,
    heat,
    held,
    outgoing,
    incoming,
    back_out,
    back_in,
    sems,
    send_sem,
    recv_sem,
):
    me = lax.axis_index("face") * 16 + lax.axis_index("elem")
    copies = load_tables(long_hbm, short_hbm, long_in, short_in, sems)
    for copy in copies:
        copy.start()
    barrier = pltpu.get_barrier_semaphore()

    def greet(step, carry):
        peer = lax.rem(me + step, PEERS)
        pl.semaphore_signal(
            barrier,
            inc=1,
            device_id=(peer // 16, lax.rem(peer, 16)),
            device_id_type=pl.DeviceIdType.MESH,
        )
        return carry

    lax.fori_loop(1, PEERS, greet, 0)
    rows_v[...] = index[...] * 4
    rows_copy = pltpu.make_async_copy(rows_v, rows, sems.at[6])
    rows_copy.start()

    slot, position = slots_of(targets[pl.ds(2 * me, 2), :])
    fields = jnp.concatenate(
        [
            thickness[...],
            amount[...],
            scatter[...],
            cloud_path[...],
            planck[...],
            as_row(cosine[...]),
            as_row(albedo[...]),
            as_row(surface[...]),
            position,
            jnp.zeros((4, COLS), jnp.float32),
        ],
        axis=0,
    )
    chooser = onehot(slot == iota((COLS, COLS), 0).astype(jnp.float32))
    packed = pick(chooser, fields, 1).reshape(PEERS, 2, 128)
    outgoing[...] = packed
    spread_weights(weights, lanes)
    pl.semaphore_wait(barrier, PEERS - 1)
    exchange(PEERS, me, outgoing, incoming, send_sem.at[0], recv_sem.at[0])
    own = pltpu.make_async_copy(outgoing.at[me], incoming.at[me], sems.at[7])
    own.start()
    for copy in copies:
        copy.wait()
    fill_table(long_in, short_in, table)
    rows_copy.wait()
    gather(rows, table, lanes, kappa)
    own.wait()
    await_all(PEERS, outgoing, incoming, send_sem.at[0], recv_sem.at[0])
    got = incoming[...].reshape(COLS, 128)
    arrived = got[:, 123:124]
    state[...] = pick(onehot(to_row(arrived) == iota((COLS, COLS), 0).astype(jnp.float32)), got)
    params = (
        two(as_row(cloud_long[...]) * 2.0),
        two(as_row(planck_part[...])),
        two(short_row(cloud_short, 0.0)),
        two(short_row(ray, 1.0)),
        two(short_row(flux, 0.0)),
    )
    radiate(state, kappa, heat, lit, params, held)
    back = onehot(arrived == iota((COLS, COLS), 1).astype(jnp.float32))
    back_out[...] = pick(back, heat[...]).reshape(PEERS, 2, 128)
    exchange(PEERS, me, back_out, back_in, send_sem.at[1], recv_sem.at[1])
    own = pltpu.make_async_copy(back_out.at[me], back_in.at[me], sems.at[7])
    own.start()
    own.wait()
    await_all(PEERS, back_out, back_in, send_sem.at[1], recv_sem.at[1])
    home = onehot(to_column(slot) == iota((COLS, COLS), 1).astype(jnp.float32))
    final = pick(home, back_in[...].reshape(COLS, 128)).T
    long_out[...] = final[:LEVELS]
    short_out[...] = final[LEVELS:2 * LEVELS]


def on_device(
    amount,
    scatter,
    cloud_path,
    planck,
    thickness,
    corner_weights,
    table_index,
    cosine,
    albedo,
    surface_source,
    stretch_map,
    sunlit,
    table_longwave,
    table_shortwave,
    cloud_longwave,
    cloud_shortwave,
    planck_fraction,
    rayleigh,
    solar_flux,
):
    anywhere = pl.BlockSpec(memory_space=pl.ANY)
    vector = pl.BlockSpec(memory_space=pltpu.VMEM)
    scalar = pl.BlockSpec(memory_space=pltpu.SMEM)
    field = jax.ShapeDtypeStruct((LEVELS, COLS), jnp.float32)
    buffer = pltpu.VMEM((PEERS, 2, 128), jnp.float32)
    return pl.pallas_call(
        column_kernel,
        out_shape=(field, field),
        in_specs=[scalar] + [vector] * 16 + [anywhere] * 2,
        out_specs=(vector, vector),
        scratch_shapes=[
            pltpu.VMEM((NTAB * 4, 128), jnp.float32),
            pltpu.VMEM((NTAB, 256), jnp.bfloat16),
            pltpu.VMEM((256, NTAB), jnp.bfloat16),
            pltpu.VMEM((LEVELS, COLS), jnp.int32),
            pltpu.SMEM((LEVELS, COLS), jnp.int32),
            pltpu.VMEM((3 * COLS, 256), jnp.float32),
            pltpu.VMEM((3 * COLS * 32, 128), jnp.float32),
            pltpu.VMEM((COLS, 128), jnp.float32),
            pltpu.VMEM((COLS, 128), jnp.float32),
            pltpu.VMEM((LEVELS, 10, WIDE, 128), jnp.float32),
            buffer,
            buffer,
            buffer,
            buffer,
            pltpu.SemaphoreType.DMA((8,)),
            pltpu.SemaphoreType.DMA((2,)),
            pltpu.SemaphoreType.DMA((2,)),
        ],
        compiler_params=pltpu.CompilerParams(
            collective_id=0, has_side_effects=True, vmem_limit_bytes=60 * 2**20
        ),
    )(
        sunlit,
        stretch_map.reshape(COLS, 128),
        amount,
        scatter,
        cloud_path,
        planck,
        thickness,
        cosine.reshape(2, 128),
        albedo.reshape(2, 128),
        surface_source.reshape(2, 128),
        corner_weights,
        table_index,
        cloud_longwave.reshape(2, 128),
        cloud_shortwave.reshape(1, 224),
        planck_fraction.reshape(2, 128),
        rayleigh.reshape(1, 224),
        solar_flux.reshape(1, 224),
        table_longwave,
        table_shortwave.T,
    )


def solution(mesh):
    columns = P(None, ("face", "elem"))
    single = P(("face", "elem"))
    in_specs = (
        (columns,) * 5
        + (P(None, None, ("face", "elem")), columns)
        + (single,) * 3
        + (P(), single)
        + (P(),) * 7
    )
    return jax.shard_map(
        on_device, mesh=mesh, in_specs=in_specs, out_specs=(columns, columns), check_vma=False
    )
```

profile of v0, /device:TPU:1, one launch (start us, length us, event | category | flops | bytes accessed | tf_op | source)
XLA Modules:
  0.0 70.0 jit_solution(16985858017641569991)
XLA Ops:
  0.6 66.7 %shard_map.194 = (f32[24,256]{1,0:T(8,128)}, f32[24,256]{1,0:T(8,128)}) custom-call(s32[2]{0:T(128)} %lit.1, s32[256,128]{1,0:T(8,128)} %bitcast.11, f32[24,256]{1,0:T(8,128)} %amount.1, f32[24,256]{1,0:T(8,128)} %scatter.1, f32[24,256]{1,0:T(8,128)} %cloud_path.1, f32[24,256]{1,0:T(8,128)} %planck.1, f32[24,256]{1,0:T(8,128)} %thickness.1, ...), custom_call_target="tpu_custom_call" | custom-call | tf_op jit(solution)/shard_map/pallas_call | solution.py:416
  67.3 1.3 %copy.23 = f32[24,256]{1,0:T(8,128)} copy(f32[24,256]{1,0:T(8,128)} %get-tuple-element.4) | data formatting | bytes 49152
  68.7 1.3 %copy.24 = f32[24,256]{1,0:T(8,128)} copy(f32[24,256]{1,0:T(8,128)} %get-tuple-element.5) | data formatting | bytes 49152
where the time goes:
time: 70.3 us; the launch traced here: 70 us
  Pallas kernels  66.7 us (95%)
  local copies, waits for them, and re-layouts  2.69 us (4%)
    pallas_call x1, Pallas kernels, on_device(): pl.pallas_call(column_kernel, out_shape=(field, field), in_specs=[scalar]...  66.7 us
    unnamed x2, local copies, waits for them, and re-layouts  2.69 us

commit v1 on v0

--- a/solution.py
+++ b/solution.py
@@ -12,11 +12,13 @@
 NT_PRES = 60
 NTAB = 7560
 COLS = 256
-PEERS = 128
 FULL = NTAB // 16 * 16
 SCALE = -0.83 / math.log(2.0)
 CORNERS = tuple(4 * (e * NT_TEMP * NT_PRES + t * NT_PRES) for e in range(2) for t in range(2))
-GROUP = 32
+GROUP = 64
+PITCH = 40
+FACES = 8
+ELEMS = 16
 WIDE = 16
 
 
@@ -120,18 +122,18 @@
 
     def body(step, carry):
         third = step // (COLS // GROUP)
-        first = step % (COLS // GROUP) * GROUP
+        origin = third * 8 * COLS + step % (COLS // GROUP) * GROUP
         for member in range(GROUP):
             place = step * GROUP + member
             picked = []
             for level in range(8):
-                base = rows[third * 8 + level, first + member]
+                base = rows[origin + (level * COLS + member)]
                 for corner in CORNERS:
                     picked.append(table[pl.ds(base + corner, 8), :])
             right = jnp.concatenate(picked, axis=0).astype(jnp.bfloat16)
             weight = jnp.broadcast_to(lanes[pl.ds(place, 1), :], (32, 256))
             left = jnp.where(mask, weight, 0.0).astype(jnp.bfloat16)
-            kappa[pl.ds(pl.multiple_of(place * 32, 32), 32), :] = jnp.dot(
+            kappa[pl.ds(pl.multiple_of(place * PITCH, 8), 32), :] = jnp.dot(
                 left, right, preferred_element_type=jnp.float32
             )
         return carry
@@ -163,16 +165,16 @@
             scatter = wide(scaled, 48 + level)
             cloud = wide(scaled, 72 + level)
             planck = wide(fields, 96 + level)
-            origin = (level // 8 * COLS + start) * 32 + level % 8 * 4
+            origin = (level // 8 * COLS + start) * PITCH + level % 8 * 4
             for half in range(2):
-                value = kappa[pl.ds(origin + half, WIDE, 32), :]
+                value = kappa[pl.ds(origin + half, WIDE, PITCH), :]
                 absorb = 1.0 - jnp.exp2(amount * value + cloud * cloud_long[half])
                 gain = absorb * (planck - down[half])
                 down[half] = down[half] + gain
                 held[level, half] = absorb
                 held[level, 2 + half] = gain
             for half in range(2):
-                value = kappa[pl.ds(origin + 2 + half, WIDE, 32), :]
+                value = kappa[pl.ds(origin + 2 + half, WIDE, PITCH), :]
                 absorbed = amount * value
                 scattered = scatter * ray[half] + cloud * cloud_short[half]
                 extinct = absorbed + scattered
@@ -205,7 +207,7 @@
             result = jnp.where(
                 lane == LEVELS + level, jnp.sum(short_sum, axis=1, keepdims=True), result
             )
-        flag = jnp.where(step < PEERS // WIDE, lit[0], lit[1]).astype(jnp.float32)
+        flag = jnp.where(step < COLS // 2 // WIDE, lit[0], lit[1]).astype(jnp.float32)
         is_long = lane < LEVELS
         thickness = jnp.where(is_long, fields, pltpu.roll(fields, LEVELS, 1))
         factor = jnp.where(is_long, -1.0 / 256.0, cosine * (flag / 224.0))
@@ -227,33 +229,25 @@
     return jnp.concatenate([row, jnp.full((1, 32), fill, jnp.float32)], axis=1)
 
 
-def exchange(count, me, outgoing, incoming, send_sem, recv_sem):
-    def copy_to(step):
+def exchange(axis, outgoing, incoming, send_sem, recv_sem):
+    count = lax.axis_size(axis)
+    me = lax.axis_index(axis)
+    for step in range(1, count):
         peer = lax.rem(me + step, count)
-        return pltpu.make_async_remote_copy(
-            src_ref=outgoing.at[peer],
-            dst_ref=incoming.at[me],
+        pltpu.make_async_remote_copy(
+            src_ref=outgoing(peer),
+            dst_ref=incoming(me),
             send_sem=send_sem,
             recv_sem=recv_sem,
-            device_id=(peer // 16, lax.rem(peer, 16)),
+            device_id={axis: peer},
             device_id_type=pl.DeviceIdType.MESH,
-        )
-
-    def start(step, carry):
-        copy_to(step).start()
-        return carry
-
-    lax.fori_loop(1, count, start, 0)
-
-
-def await_all(count, outgoing, incoming, send_sem, recv_sem):
-    most = count - 1
-    pltpu.make_async_copy(
-        outgoing.at[pl.ds(0, most)], incoming.at[pl.ds(0, most)], send_sem
-    ).wait()
-    pltpu.make_async_copy(
-        outgoing.at[pl.ds(0, most)], incoming.at[pl.ds(0, most)], recv_sem
-    ).wait()
+        ).start()
+
+
+def await_all(axis, buffer, send_sem, recv_sem):
+    whole = buffer.at[pl.ds(0, lax.axis_size(axis) - 1)]
+    pltpu.make_async_copy(whole, whole, send_sem).wait()
+    pltpu.make_async_copy(whole, whole, recv_sem).wait()
 
 
 def load_tables(long_hbm, short_hbm, long_in, short_in, sems):
@@ -291,8 +285,8 @@
     flux,
     long_hbm,
     short_hbm,
-    long_out,
-    short_out,
+    returned,
+    slot_out,
     table,
     long_in,
     short_in,
@@ -304,33 +298,37 @@
     heat,
     held,
     outgoing,
+    middle,
     incoming,
     back_out,
-    back_in,
+    back_middle,
     sems,
     send_sem,
     recv_sem,
 ):
-    me = lax.axis_index("face") * 16 + lax.axis_index("elem")
+    me = lax.axis_index("face") * ELEMS + lax.axis_index("elem")
     copies = load_tables(long_hbm, short_hbm, long_in, short_in, sems)
     for copy in copies:
         copy.start()
+    face = lax.axis_index("face")
+    elem = lax.axis_index("elem")
     barrier = pltpu.get_barrier_semaphore()
-
-    def greet(step, carry):
-        peer = lax.rem(me + step, PEERS)
-        pl.semaphore_signal(
-            barrier,
-            inc=1,
-            device_id=(peer // 16, lax.rem(peer, 16)),
-            device_id_type=pl.DeviceIdType.MESH,
-        )
-        return carry
-
-    lax.fori_loop(1, PEERS, greet, 0)
+    for axis, count in (("face", FACES), ("elem", ELEMS)):
+        for step in range(1, count):
+            pl.semaphore_signal(
+                barrier,
+                inc=1,
+                device_id={axis: lax.rem(lax.axis_index(axis) + step, count)},
+                device_id_type=pl.DeviceIdType.MESH,
+            )
     rows_v[...] = index[...] * 4
-    rows_copy = pltpu.make_async_copy(rows_v, rows, sems.at[6])
-    rows_copy.start()
+    row_copies = []
+    for level in range(LEVELS):
+        row_copies.append(
+            pltpu.make_async_copy(rows_v.at[level], rows.at[pl.ds(level * COLS, COLS)], sems.at[6])
+        )
+    for copy in row_copies:
+        copy.start()
 
     slot, position = slots_of(targets[pl.ds(2 * me, 2), :])
     fields = jnp.concatenate(
@@ -349,20 +347,30 @@
         axis=0,
     )
     chooser = onehot(slot == iota((COLS, COLS), 0).astype(jnp.float32))
-    packed = pick(chooser, fields, 1).reshape(PEERS, 2, 128)
-    outgoing[...] = packed
+    slot_out[...] = slot
+    outgoing[...] = pick(chooser, fields, 1).reshape(FACES, ELEMS, 2, 128)
+    own = pltpu.make_async_copy(outgoing.at[face], middle.at[face], sems.at[7])
+    own.start()
     spread_weights(weights, lanes)
-    pl.semaphore_wait(barrier, PEERS - 1)
-    exchange(PEERS, me, outgoing, incoming, send_sem.at[0], recv_sem.at[0])
-    own = pltpu.make_async_copy(outgoing.at[me], incoming.at[me], sems.at[7])
-    own.start()
+    pl.semaphore_wait(barrier, FACES + ELEMS - 2)
+    exchange(
+        "face", lambda k: outgoing.at[k], lambda k: middle.at[k], send_sem.at[0], recv_sem.at[0]
+    )
     for copy in copies:
         copy.wait()
     fill_table(long_in, short_in, table)
-    rows_copy.wait()
+    own.wait()
+    await_all("face", middle, send_sem.at[0], recv_sem.at[0])
+    exchange(
+        "elem", lambda k: middle.at[:, k], lambda k: incoming.at[k], send_sem.at[1], recv_sem.at[1]
+    )
+    own = pltpu.make_async_copy(middle.at[:, elem], incoming.at[elem], sems.at[7])
+    own.start()
+    for copy in row_copies:
+        copy.wait()
     gather(rows, table, lanes, kappa)
     own.wait()
-    await_all(PEERS, outgoing, incoming, send_sem.at[0], recv_sem.at[0])
+    await_all("elem", incoming, send_sem.at[1], recv_sem.at[1])
     got = incoming[...].reshape(COLS, 128)
     arrived = got[:, 123:124]
     state[...] = pick(onehot(to_row(arrived) == iota((COLS, COLS), 0).astype(jnp.float32)), got)
@@ -375,14 +383,26 @@
     )
     radiate(state, kappa, heat, lit, params, held)
     back = onehot(arrived == iota((COLS, COLS), 1).astype(jnp.float32))
-    back_out[...] = pick(back, heat[...]).reshape(PEERS, 2, 128)
-    exchange(PEERS, me, back_out, back_in, send_sem.at[1], recv_sem.at[1])
-    own = pltpu.make_async_copy(back_out.at[me], back_in.at[me], sems.at[7])
+    back_out[...] = pick(back, heat[...]).reshape(ELEMS, FACES, 2, 128)
+    own = pltpu.make_async_copy(back_out.at[elem], back_middle.at[:, elem], sems.at[7])
+    own.start()
+    exchange(
+        "elem", lambda k: back_out.at[k], lambda k: back_middle.at[:, k], send_sem.at[2], recv_sem.at[2]
+    )
+    own.wait()
+    await_all("elem", back_out, send_sem.at[2], recv_sem.at[2])
+    exchange(
+        "face", lambda k: back_middle.at[k], lambda k: returned.at[k], send_sem.at[3], recv_sem.at[3]
+    )
+    own = pltpu.make_async_copy(back_middle.at[face], returned.at[face], sems.at[7])
     own.start()
     own.wait()
-    await_all(PEERS, back_out, back_in, send_sem.at[1], recv_sem.at[1])
-    home = onehot(to_column(slot) == iota((COLS, COLS), 1).astype(jnp.float32))
-    final = pick(home, back_in[...].reshape(COLS, 128)).T
+    await_all("face", back_middle, send_sem.at[3], recv_sem.at[3])
+
+
+def home_kernel(returned, slot, long_out, short_out):
+    home = onehot(to_column(slot[...]) == iota((COLS, COLS), 1).astype(jnp.float32))
+    final = pick(home, returned[...].reshape(COLS, 128)).T
     long_out[...] = final[:LEVELS]
     short_out[...] = final[LEVELS:2 * LEVELS]
 
@@ -412,30 +432,35 @@
     vector = pl.BlockSpec(memory_space=pltpu.VMEM)
     scalar = pl.BlockSpec(memory_space=pltpu.SMEM)
     field = jax.ShapeDtypeStruct((LEVELS, COLS), jnp.float32)
-    buffer = pltpu.VMEM((PEERS, 2, 128), jnp.float32)
-    return pl.pallas_call(
+    by_face = pltpu.VMEM((FACES, ELEMS, 2, 128), jnp.float32)
+    by_elem = pltpu.VMEM((ELEMS, FACES, 2, 128), jnp.float32)
+    returned, slot = pl.pallas_call(
         column_kernel,
-        out_shape=(field, field),
+        out_shape=(
+            jax.ShapeDtypeStruct((FACES, ELEMS, 2, 128), jnp.float32),
+            jax.ShapeDtypeStruct((1, COLS), jnp.float32),
+        ),
         in_specs=[scalar] + [vector] * 16 + [anywhere] * 2,
-        out_specs=(vector, vector),
+        out_specs=(anywhere, vector),
         scratch_shapes=[
             pltpu.VMEM((NTAB * 4, 128), jnp.float32),
             pltpu.VMEM((NTAB, 256), jnp.bfloat16),
             pltpu.VMEM((256, NTAB), jnp.bfloat16),
             pltpu.VMEM((LEVELS, COLS), jnp.int32),
-            pltpu.SMEM((LEVELS, COLS), jnp.int32),
+            pltpu.SMEM((LEVELS * COLS,), jnp.int32),
             pltpu.VMEM((3 * COLS, 256), jnp.float32),
-            pltpu.VMEM((3 * COLS * 32, 128), jnp.float32),
+            pltpu.VMEM((3 * COLS * PITCH, 128), jnp.float32),
             pltpu.VMEM((COLS, 128), jnp.float32),
             pltpu.VMEM((COLS, 128), jnp.float32),
             pltpu.VMEM((LEVELS, 10, WIDE, 128), jnp.float32),
-            buffer,
-            buffer,
-            buffer,
-            buffer,
+            by_face,
+            by_face,
+            by_elem,
+            by_elem,
+            by_face,
             pltpu.SemaphoreType.DMA((8,)),
-            pltpu.SemaphoreType.DMA((2,)),
-            pltpu.SemaphoreType.DMA((2,)),
+            pltpu.SemaphoreType.DMA((4,)),
+            pltpu.SemaphoreType.DMA((4,)),
         ],
         compiler_params=pltpu.CompilerParams(
             collective_id=0, has_side_effects=True, vmem_limit_bytes=60 * 2**20
@@ -461,6 +486,12 @@
         table_longwave,
         table_shortwave.T,
     )
+    return pl.pallas_call(
+        home_kernel,
+        out_shape=(field, field),
+        in_specs=[vector, vector],
+        out_specs=(vector, vector),
+    )(returned, slot)
 
 
 def solution(mesh):

time: 70.3 us -> 55.6 us (0.79)
  Pallas kernels: 66.7 us -> 54.8 us
  local copies, waits for them, and re-layouts: 2.69 us -> 0 us
    pallas_call x1 -> x2, Pallas kernels: 66.7 us -> 54.8 us  [the longest x1 52.9 us: on_device(): pl.pallas_call(column_kernel, out_shape=(jax.ShapeDtypeStruct((FACES, ELE...]
    unnamed x2 -> x0, local copies, waits for them, and re-layouts: 2.69 us -> none
where the time goes in v1:
time: 55.6 us; the launch traced here: 55.5 us
  Pallas kernels  54.8 us (99%)
  between operations  0.65 us (1%)
    pallas_call x1, Pallas kernels, on_device(): pl.pallas_call(column_kernel, out_shape=(jax.ShapeDtypeStruct((FACES, ELE...  52.9 us
    pallas_call x1, Pallas kernels, on_device(): pl.pallas_call(home_kernel, out_shape=(field, field), in_specs=[vector, v...  1.97 us

profile of v1, /device:TPU:1, one launch (start us, length us, event | category | flops | bytes accessed | tf_op | source)
XLA Modules:
  0.0 55.5 jit_solution(15685764292387538772)
XLA Ops:
  0.6 52.9 %shard_map.194 = (f32[8,16,2,128]{3,2,1,0:T(2,128)}, f32[1,256]{1,0:T(1,128)}) custom-call(s32[2]{0:T(128)} %lit.1, s32[256,128]{1,0:T(8,128)} %bitcast.11, f32[24,256]{1,0:T(8,128)} %amount.1, f32[24,256]{1,0:T(8,128)} %scatter.1, f32[24,256]{1,0:T(8,128)} %cloud_path.1, f32[24,256]{1,0:T(8,128)} %planck.1, f32[24,256]{1,0:T(8,128)} %thickness.1, ...), custom_call_target="tpu_custom_call" | custom-call | tf_op jit(solution)/shard_map/pallas_call | solution.py:437
  53.5 2.0 %shard_map.195 = (f32[24,256]{1,0:T(8,128)}, f32[24,256]{1,0:T(8,128)}) custom-call(f32[8,16,2,128]{3,2,1,0:T(2,128)} %get-tuple-element.4.returned, f32[1,256]{1,0:T(1,128)} %get-tuple-element.5.slot), custom_call_target="tpu_custom_call" | custom-call | tf_op jit(solution)/shard_map/pallas_call | solution.py:489

commit v2 on v1

--- a/solution.py
+++ b/solution.py
@@ -73,37 +73,38 @@
     return 2.0 * owner + rank, position
 
 
-def fill_table(long_in, short_in, table):
-    def long_rows(base, count):
+def fill_long(long_in, table):
+    def rows_at(base, count):
         rows = long_in[pl.ds(base, count), :].astype(jnp.float32) * 2.0
         table[pl.ds(base * 4, count, 4), :] = rows[:, :128]
         table[pl.ds(base * 4 + 1, count, 4), :] = rows[:, 128:]
 
-    def long_body(step, carry):
+    def body(step, carry):
         for inner in range(8):
-            long_rows(pl.multiple_of(step * 128, 128) + inner * 16, 16)
+            rows_at(pl.multiple_of(step * 128, 128) + inner * 16, 16)
         return carry
 
-    lax.fori_loop(0, FULL // 128, long_body, 0)
-    long_rows(FULL, NTAB - FULL)
-
-    def short_rows(block, base, count):
-        unit = onehot(iota((count, count), 0) == iota((count, count), 1))
-        rows = lax.dot_general(
-            unit, block, (((1,), (1,)), ((), ())), preferred_element_type=jnp.float32
-        )
+    lax.fori_loop(0, FULL // 128, body, 0)
+    rows_at(FULL, NTAB - FULL)
+
+
+def fill_short(short_in, table):
+    def rows_at(block, base, count):
+        rows = block.astype(jnp.float32).T
         table[pl.ds(base * 4 + 2, count, 4), :] = rows[:, :128]
         table[pl.ds(base * 4 + 3, count, 4), :] = rows[:, 128:]
 
-    def short_body(step, carry):
-        base = pl.multiple_of(step * 256, 256)
-        short_rows(short_in[:, pl.ds(base, 256)], base, 256)
+    def body(step, carry):
+        for inner in range(4):
+            base = pl.multiple_of(step * 1024, 256) + inner * 256
+            rows_at(short_in[:, pl.ds(base, 256)], base, 256)
         return carry
 
     short_in[224:256, :] = jnp.zeros((32, NTAB), jnp.bfloat16)
-    lax.fori_loop(0, NTAB // 256, short_body, 0)
-    short_rows(short_in[:, FULL - 128:FULL], FULL - 128, 128)
-    short_rows(short_in[:, FULL:NTAB], FULL, NTAB - FULL)
+    lax.fori_loop(0, NTAB // 1024, body, 0)
+    for base in range(NTAB // 1024 * 1024, FULL, 128):
+        rows_at(short_in[:, base:base + 128], base, 128)
+    rows_at(short_in[:, FULL:NTAB], FULL, NTAB - FULL)
 
 
 def spread_weights(weights, lanes):
@@ -116,7 +117,7 @@
         )
 
 
-def gather(rows, table, lanes, kappa):
+def gather(rows, table, lanes, kappa, first, last):
     out_row, lane = iota((32, 256), 0), iota((32, 256), 1)
     mask = (out_row // 4 == lane // 32) & (out_row % 4 == lane % 4)
 
@@ -138,7 +139,7 @@
             )
         return carry
 
-    lax.fori_loop(0, 3 * COLS // GROUP, body, 0)
+    lax.fori_loop(first, last, body, 0)
 
 
 def radiate(state, kappa, heat, lit, params, held):
@@ -301,7 +302,7 @@
     middle,
     incoming,
     back_out,
-    back_middle,
+    arrival,
     sems,
     send_sem,
     recv_sem,
@@ -352,13 +353,20 @@
     own = pltpu.make_async_copy(outgoing.at[face], middle.at[face], sems.at[7])
     own.start()
     spread_weights(weights, lanes)
+    for copy in copies[:4]:
+        copy.wait()
+    fill_long(long_in, table)
     pl.semaphore_wait(barrier, FACES + ELEMS - 2)
     exchange(
         "face", lambda k: outgoing.at[k], lambda k: middle.at[k], send_sem.at[0], recv_sem.at[0]
     )
-    for copy in copies:
+    for copy in copies[4:]:
         copy.wait()
-    fill_table(long_in, short_in, table)
+    fill_short(short_in, table)
+    for copy in row_copies:
+        copy.wait()
+    steps = 3 * COLS // GROUP
+    gather(rows, table, lanes, kappa, 0, steps // 2)
     own.wait()
     await_all("face", middle, send_sem.at[0], recv_sem.at[0])
     exchange(
@@ -366,13 +374,12 @@
     )
     own = pltpu.make_async_copy(middle.at[:, elem], incoming.at[elem], sems.at[7])
     own.start()
-    for copy in row_copies:
-        copy.wait()
-    gather(rows, table, lanes, kappa)
+    gather(rows, table, lanes, kappa, steps // 2, steps)
     own.wait()
     await_all("elem", incoming, send_sem.at[1], recv_sem.at[1])
     got = incoming[...].reshape(COLS, 128)
     arrived = got[:, 123:124]
+    arrival[...] = got
     state[...] = pick(onehot(to_row(arrived) == iota((COLS, COLS), 0).astype(jnp.float32)), got)
     params = (
         two(as_row(cloud_long[...]) * 2.0),
@@ -382,27 +389,49 @@
         two(short_row(flux, 0.0)),
     )
     radiate(state, kappa, heat, lit, params, held)
-    back = onehot(arrived == iota((COLS, COLS), 1).astype(jnp.float32))
-    back_out[...] = pick(back, heat[...]).reshape(ELEMS, FACES, 2, 128)
-    own = pltpu.make_async_copy(back_out.at[elem], back_middle.at[:, elem], sems.at[7])
+    for rank in range(2):
+        there = arrival[pl.ds(rank, COLS // 2, 2), :][:, 123:124]
+        back = onehot(there == iota((COLS // 2, COLS), 1).astype(jnp.float32))
+        found = pick(back, heat[...])
+        both = found if rank == 0 else both + pltpu.roll(found, 64, 1)
+    back_out[...] = both.reshape(COLS // 2, 1, 128)
+    own = pltpu.make_async_copy(
+        back_out.at[elem * FACES + face], returned.at[me], sems.at[7]
+    )
     own.start()
-    exchange(
-        "elem", lambda k: back_out.at[k], lambda k: back_middle.at[:, k], send_sem.at[2], recv_sem.at[2]
-    )
+
+    def send_one(step):
+        peer = (me + step) & (FACES * ELEMS - 1)
+        to_face = peer >> 4
+        to_elem = peer & 15
+        pltpu.make_async_remote_copy(
+            src_ref=back_out.at[to_elem * FACES + to_face],
+            dst_ref=returned.at[me],
+            send_sem=send_sem.at[2],
+            recv_sem=recv_sem.at[2],
+            device_id=(to_face, to_elem),
+            device_id_type=pl.DeviceIdType.MESH,
+        ).start()
+
+    def send_home(group, carry):
+        for inner in range(9):
+            send_one(group * 9 + inner + 1)
+        return carry
+
+    lax.fori_loop(0, 14, send_home, 0)
+    send_one(127)
     own.wait()
-    await_all("elem", back_out, send_sem.at[2], recv_sem.at[2])
-    exchange(
-        "face", lambda k: back_middle.at[k], lambda k: returned.at[k], send_sem.at[3], recv_sem.at[3]
-    )
-    own = pltpu.make_async_copy(back_middle.at[face], returned.at[face], sems.at[7])
-    own.start()
-    own.wait()
-    await_all("face", back_middle, send_sem.at[3], recv_sem.at[3])
+    most = back_out.at[pl.ds(0, FACES * ELEMS - 1)]
+    pltpu.make_async_copy(most, most, send_sem.at[2]).wait()
+    pltpu.make_async_copy(most, most, recv_sem.at[2]).wait()
 
 
 def home_kernel(returned, slot, long_out, short_out):
-    home = onehot(to_column(slot[...]) == iota((COLS, COLS), 1).astype(jnp.float32))
-    final = pick(home, returned[...].reshape(COLS, 128)).T
+    place = to_column(slot[...])
+    peer = jnp.floor(place * 0.5)
+    home = onehot(peer == iota((COLS, COLS // 2), 1).astype(jnp.float32))
+    both = pick(home, returned[...].reshape(COLS // 2, 128))
+    final = jnp.where(place > 2.0 * peer, pltpu.roll(both, 64, 1), both).T
     long_out[...] = final[:LEVELS]
     short_out[...] = final[LEVELS:2 * LEVELS]
 
@@ -437,7 +466,7 @@
     returned, slot = pl.pallas_call(
         column_kernel,
         out_shape=(
-            jax.ShapeDtypeStruct((FACES, ELEMS, 2, 128), jnp.float32),
+            jax.ShapeDtypeStruct((COLS // 2, 1, 128), jnp.float32),
             jax.ShapeDtypeStruct((1, COLS), jnp.float32),
         ),
         in_specs=[scalar] + [vector] * 16 + [anywhere] * 2,
@@ -456,11 +485,11 @@
             by_face,
             by_face,
             by_elem,
-            by_elem,
-            by_face,
+            pltpu.VMEM((COLS // 2, 1, 128), jnp.float32),
+            pltpu.VMEM((COLS, 128), jnp.float32),
             pltpu.SemaphoreType.DMA((8,)),
-            pltpu.SemaphoreType.DMA((4,)),
-            pltpu.SemaphoreType.DMA((4,)),
+            pltpu.SemaphoreType.DMA((3,)),
+            pltpu.SemaphoreType.DMA((3,)),
         ],
         compiler_params=pltpu.CompilerParams(
             collective_id=0, has_side_effects=True, vmem_limit_bytes=60 * 2**20

time: 55.6 us -> 47.7 us (0.86)
  Pallas kernels: 54.8 us -> 46.9 us
    pallas_call x1, Pallas kernels: 52.9 us -> 44.9 us  [on_device(): pl.pallas_call(column_kernel, out_shape=(jax.ShapeDtypeStruct((COLS // 2,...]
where the time goes in v2:
time: 47.7 us; the launch traced here: 47.6 us
  Pallas kernels  46.9 us (98%)
  between operations  0.65 us (1%)
    pallas_call x1, Pallas kernels, on_device(): pl.pallas_call(column_kernel, out_shape=(jax.ShapeDtypeStruct((COLS // 2,...  44.9 us
    pallas_call x1, Pallas kernels, on_device(): pl.pallas_call(home_kernel, out_shape=(field, field), in_specs=[vector, v...  2.05 us

profile of v2, /device:TPU:1, one launch (start us, length us, event | category | flops | bytes accessed | tf_op | source)
XLA Modules:
  0.0 47.6 jit_solution(3007571361566170124)
XLA Ops:
  0.6 44.9 %shard_map.194 = (f32[128,1,128]{2,1,0:T(1,128)}, f32[1,256]{1,0:T(1,128)}) custom-call(s32[2]{0:T(128)} %lit.1, s32[256,128]{1,0:T(8,128)} %bitcast.11, f32[24,256]{1,0:T(8,128)} %amount.1, f32[24,256]{1,0:T(8,128)} %scatter.1, f32[24,256]{1,0:T(8,128)} %cloud_path.1, f32[24,256]{1,0:T(8,128)} %planck.1, f32[24,256]{1,0:T(8,128)} %thickness.1, ...), custom_call_target="tpu_custom_call" | custom-call | tf_op jit(solution)/shard_map/pallas_call | solution.py:466
  45.5 2.0 %shard_map.195 = (f32[24,256]{1,0:T(8,128)}, f32[24,256]{1,0:T(8,128)}) custom-call(f32[128,1,128]{2,1,0:T(1,128)} %get-tuple-element.4.returned, f32[1,256]{1,0:T(1,128)} %get-tuple-element.5.slot), custom_call_target="tpu_custom_call" | custom-call | tf_op jit(solution)/shard_map/pallas_call | solution.py:518

commit v3 on v2

--- a/solution.py
+++ b/solution.py
@@ -13,13 +13,14 @@
 NTAB = 7560
 COLS = 256
 FULL = NTAB // 16 * 16
-SCALE = -0.83 / math.log(2.0)
+SCALE = -1.66 / math.log(2.0)
+SHORT_AT = 32
 CORNERS = tuple(4 * (e * NT_TEMP * NT_PRES + t * NT_PRES) for e in range(2) for t in range(2))
-GROUP = 64
-PITCH = 40
+GROUP = 128
+PITCH = 8
 FACES = 8
 ELEMS = 16
-WIDE = 16
+WIDE = 32
 
 
 def iota(shape, axis):
@@ -75,7 +76,7 @@
 
 def fill_long(long_in, table):
     def rows_at(base, count):
-        rows = long_in[pl.ds(base, count), :].astype(jnp.float32) * 2.0
+        rows = long_in[pl.ds(base, count), :].astype(jnp.float32)
         table[pl.ds(base * 4, count, 4), :] = rows[:, :128]
         table[pl.ds(base * 4 + 1, count, 4), :] = rows[:, 128:]
 
@@ -112,31 +113,42 @@
     expand = onehot((source // 8 == (lane // 4) % 8) & (source % 8 == lane // 32))
     for third in range(3):
         low = weights[:, third * 8:third * 8 + 8, :].reshape(64, COLS).astype(jnp.bfloat16)
-        lanes[third * COLS:(third + 1) * COLS, :] = lax.dot_general(
+        spread = lax.dot_general(
             low, expand, (((0,), (0,)), ((), ())), preferred_element_type=jnp.float32
         )
+        for half in range(2):
+            lanes[half, third * COLS:(third + 1) * COLS, :] = spread[:, half * 128:half * 128 + 128]
 
 
 def gather(rows, table, lanes, kappa, first, last):
-    out_row, lane = iota((32, 256), 0), iota((32, 256), 1)
-    mask = (out_row // 4 == lane // 32) & (out_row % 4 == lane % 4)
+    out_row, lane = iota((32, 128), 0), iota((32, 128), 1)
+    mask = [
+        (out_row // 4 == lane // 32 + 4 * half) & (out_row % 4 == lane % 4) for half in range(2)
+    ]
 
     def body(step, carry):
         third = step // (COLS // GROUP)
-        origin = third * 8 * COLS + step % (COLS // GROUP) * GROUP
+        first = step % (COLS // GROUP) * GROUP
+        origin = third * 8 * COLS + first
         for member in range(GROUP):
-            place = step * GROUP + member
             picked = []
             for level in range(8):
                 base = rows[origin + (level * COLS + member)]
                 for corner in CORNERS:
                     picked.append(table[pl.ds(base + corner, 8), :])
             right = jnp.concatenate(picked, axis=0).astype(jnp.bfloat16)
-            weight = jnp.broadcast_to(lanes[pl.ds(place, 1), :], (32, 256))
-            left = jnp.where(mask, weight, 0.0).astype(jnp.bfloat16)
-            kappa[pl.ds(pl.multiple_of(place * PITCH, 8), 32), :] = jnp.dot(
-                left, right, preferred_element_type=jnp.float32
-            )
+            row = pl.ds(pl.multiple_of(step * GROUP, GROUP) + member, 1)
+            left = jnp.concatenate(
+                [
+                    jnp.where(mask[half], jnp.broadcast_to(lanes[half, row, :], (32, 128)), 0.0)
+                    for half in range(2)
+                ],
+                axis=1,
+            ).astype(jnp.bfloat16)
+            found = jnp.dot(left, right, preferred_element_type=jnp.float32)
+            for pair in range(4):
+                spot = ((third * 4 + pair) * COLS + first + member) * PITCH
+                kappa[pl.ds(pl.multiple_of(spot, 8), 8), :] = found[pair * 8:pair * 8 + 8]
         return carry
 
     lax.fori_loop(first, last, body, 0)
@@ -157,7 +169,7 @@
         cosine = wide(fields, 120)
         albedo = wide(fields, 121)
         surface = wide(fields, 122)
-        path = (1.0 / 0.83) / cosine
+        path = (1.0 / 1.66) / cosine
         down = [jnp.zeros((WIDE, 128), jnp.float32) for _ in range(2)]
         sdown = [jnp.zeros((WIDE, 128), jnp.float32) for _ in range(2)]
         direct = [jnp.ones((WIDE, 128), jnp.float32) for _ in range(2)]
@@ -166,53 +178,58 @@
             scatter = wide(scaled, 48 + level)
             cloud = wide(scaled, 72 + level)
             planck = wide(fields, 96 + level)
-            origin = (level // 8 * COLS + start) * PITCH + level % 8 * 4
+            origin = (level // 2 * COLS + start) * PITCH + level % 2 * 4
             for half in range(2):
                 value = kappa[pl.ds(origin + half, WIDE, PITCH), :]
-                absorb = 1.0 - jnp.exp2(amount * value + cloud * cloud_long[half])
-                gain = absorb * (planck - down[half])
-                down[half] = down[half] + gain
-                held[level, half] = absorb
-                held[level, 2 + half] = gain
+                transmit = jnp.exp2(amount * value + cloud * cloud_long[half])
+                held[level, half] = transmit
+                held[level, 2 + half] = down[half]
+                down[half] = planck + transmit * (down[half] - planck)
             for half in range(2):
                 value = kappa[pl.ds(origin + 2 + half, WIDE, PITCH), :]
                 absorbed = amount * value
                 scattered = scatter * ray[half] + cloud * cloud_short[half]
-                extinct = absorbed + scattered
-                lost = direct[half] * (1.0 - jnp.exp2(extinct * path))
-                direct[half] = direct[half] - lost
-                kept = lost * (absorbed / extinct)
-                source = 0.5 * (lost - kept)
-                close = 1.0 - jnp.exp2(extinct + absorbed)
-                taken = close * sdown[half]
-                sdown[half] = sdown[half] - taken + source
-                held[level, 4 + half] = close
+                partial = absorbed + scattered
+                extinct = partial + scattered
+                onward = direct[half] * jnp.exp2(extinct * path)
+                source = (direct[half] - onward) * (scattered / extinct)
+                spread = jnp.exp2(partial)
+                held[level, 4 + half] = spread
                 held[level, 6 + half] = source
-                held[level, 8 + half] = taken + kept
+                held[level, 8 + half] = direct[half] + sdown[half]
+                direct[half] = onward
+                sdown[half] = spread * sdown[half] + source
         up = [surface, surface]
-        sup = [albedo * (direct[half] + sdown[half]) for half in range(2)]
+        below = [direct[half] + sdown[half] for half in range(2)]
+        sup = [albedo * below[half] for half in range(2)]
         result = jnp.zeros((WIDE, 128), jnp.float32)
+
+        def settle(result, face, upper, shorter):
+            long_net = [(up[half] - upper[half]) * planck_part[half] for half in range(2)]
+            short_net = [(sup[half] - shorter[half]) * flux[half] for half in range(2)]
+            long_sum = jnp.sum(long_net[0] + long_net[1], axis=1, keepdims=True)
+            short_sum = jnp.sum(short_net[0] + short_net[1], axis=1, keepdims=True)
+            result = jnp.where(lane == face, long_sum, result)
+            return jnp.where(lane == SHORT_AT + face, short_sum, result)
+
+        result = settle(result, LEVELS, down, below)
         for level in reversed(range(LEVELS)):
             planck = wide(fields, 96 + level)
-            long_sum, short_sum = None, None
             for half in range(2):
-                gain = held[level, half] * (planck - up[half])
-                up[half] = up[half] + gain
-                term = (gain + held[level, 2 + half]) * planck_part[half]
-                long_sum = term if half == 0 else long_sum + term
-                taken = held[level, 4 + half] * sup[half]
-                sup[half] = sup[half] - taken + held[level, 6 + half]
-                term = (taken + held[level, 8 + half]) * flux[half]
-                short_sum = term if half == 0 else short_sum + term
-            result = jnp.where(lane == level, jnp.sum(long_sum, axis=1, keepdims=True), result)
-            result = jnp.where(
-                lane == LEVELS + level, jnp.sum(short_sum, axis=1, keepdims=True), result
+                up[half] = planck + held[level, half] * (up[half] - planck)
+                sup[half] = held[level, 4 + half] * sup[half] + held[level, 6 + half]
+            result = settle(
+                result,
+                level,
+                [held[level, 2 + half] for half in range(2)],
+                [held[level, 8 + half] for half in range(2)],
             )
+        result = pltpu.roll(result, 127, 1) - result
         flag = jnp.where(step < COLS // 2 // WIDE, lit[0], lit[1]).astype(jnp.float32)
-        is_long = lane < LEVELS
-        thickness = jnp.where(is_long, fields, pltpu.roll(fields, LEVELS, 1))
-        factor = jnp.where(is_long, -1.0 / 256.0, cosine * (flag / 224.0))
-        keep = lane < 2 * LEVELS
+        is_long = lane < SHORT_AT
+        thickness = jnp.where(is_long, fields, pltpu.roll(fields, SHORT_AT, 1))
+        factor = jnp.where(is_long, 1.0 / 256.0, cosine * (flag / 224.0))
+        keep = (lane % SHORT_AT < LEVELS) & (lane < 2 * SHORT_AT)
         heat[pl.ds(start, WIDE), :] = jnp.where(
             keep, result * factor / jnp.where(keep, thickness, 1.0), 0.0
         )
@@ -382,10 +399,10 @@
     arrival[...] = got
     state[...] = pick(onehot(to_row(arrived) == iota((COLS, COLS), 0).astype(jnp.float32)), got)
     params = (
-        two(as_row(cloud_long[...]) * 2.0),
+        two(as_row(cloud_long[...])),
         two(as_row(planck_part[...])),
-        two(short_row(cloud_short, 0.0)),
-        two(short_row(ray, 1.0)),
+        two(short_row(cloud_short, 0.0) * 0.5),
+        two(short_row(ray, 1.0) * 0.5),
         two(short_row(flux, 0.0)),
     )
     radiate(state, kappa, heat, lit, params, held)
@@ -433,7 +450,7 @@
     both = pick(home, returned[...].reshape(COLS // 2, 128))
     final = jnp.where(place > 2.0 * peer, pltpu.roll(both, 64, 1), both).T
     long_out[...] = final[:LEVELS]
-    short_out[...] = final[LEVELS:2 * LEVELS]
+    short_out[...] = final[SHORT_AT:SHORT_AT + LEVELS]
 
 
 def on_device(
@@ -477,8 +494,8 @@
             pltpu.VMEM((256, NTAB), jnp.bfloat16),
             pltpu.VMEM((LEVELS, COLS), jnp.int32),
             pltpu.SMEM((LEVELS * COLS,), jnp.int32),
-            pltpu.VMEM((3 * COLS, 256), jnp.float32),
-            pltpu.VMEM((3 * COLS * PITCH, 128), jnp.float32),
+            pltpu.VMEM((2, 3 * COLS, 128), jnp.float32),
+            pltpu.VMEM((12 * COLS * PITCH, 128), jnp.float32),
             pltpu.VMEM((COLS, 128), jnp.float32),
             pltpu.VMEM((COLS, 128), jnp.float32),
             pltpu.VMEM((LEVELS, 10, WIDE, 128), jnp.float32),

time: 47.7 us -> 43.7 us (0.916)
  Pallas kernels: 46.9 us -> 42.9 us
    pallas_call x1, Pallas kernels: 44.9 us -> 40.9 us  [on_device(): pl.pallas_call(column_kernel, out_shape=(jax.ShapeDtypeStruct((COLS // 2,...]
where the time goes in v3:
time: 43.7 us; the launch traced here: 43.6 us
  Pallas kernels  42.9 us (98%)
  between operations  0.65 us (1%)
    pallas_call x1, Pallas kernels, on_device(): pl.pallas_call(column_kernel, out_shape=(jax.ShapeDtypeStruct((COLS // 2,...  40.9 us
    pallas_call x1, Pallas kernels, on_device(): pl.pallas_call(home_kernel, out_shape=(field, field), in_specs=[vector, v...  2.05 us

profile of v3, /device:TPU:1, one launch (start us, length us, event | category | flops | bytes accessed | tf_op | source)
XLA Modules:
  0.0 43.6 jit_solution(2941687609703283303)
XLA Ops:
  0.6 40.9 %shard_map.194 = (f32[128,1,128]{2,1,0:T(1,128)}, f32[1,256]{1,0:T(1,128)}) custom-call(s32[2]{0:T(128)} %lit.1, s32[256,128]{1,0:T(8,128)} %bitcast.11, f32[24,256]{1,0:T(8,128)} %amount.1, f32[24,256]{1,0:T(8,128)} %scatter.1, f32[24,256]{1,0:T(8,128)} %cloud_path.1, f32[24,256]{1,0:T(8,128)} %planck.1, f32[24,256]{1,0:T(8,128)} %thickness.1, ...), custom_call_target="tpu_custom_call" | custom-call | tf_op jit(solution)/shard_map/pallas_call | solution.py:483
  41.5 2.0 %shard_map.195 = (f32[24,256]{1,0:T(8,128)}, f32[24,256]{1,0:T(8,128)}) custom-call(f32[128,1,128]{2,1,0:T(1,128)} %get-tuple-element.4.returned, f32[1,256]{1,0:T(1,128)} %get-tuple-element.5.slot), custom_call_target="tpu_custom_call" | custom-call | tf_op jit(solution)/shard_map/pallas_call | solution.py:535

commit v4 on v3

--- a/solution.py
+++ b/solution.py
@@ -172,7 +172,7 @@
         path = (1.0 / 1.66) / cosine
         down = [jnp.zeros((WIDE, 128), jnp.float32) for _ in range(2)]
         sdown = [jnp.zeros((WIDE, 128), jnp.float32) for _ in range(2)]
-        direct = [jnp.ones((WIDE, 128), jnp.float32) for _ in range(2)]
+        direct = list(flux)
         for level in range(LEVELS):
             amount = wide(scaled, 24 + level)
             scatter = wide(scaled, 48 + level)
@@ -206,7 +206,7 @@
 
         def settle(result, face, upper, shorter):
             long_net = [(up[half] - upper[half]) * planck_part[half] for half in range(2)]
-            short_net = [(sup[half] - shorter[half]) * flux[half] for half in range(2)]
+            short_net = [sup[half] - shorter[half] for half in range(2)]
             long_sum = jnp.sum(long_net[0] + long_net[1], axis=1, keepdims=True)
             short_sum = jnp.sum(short_net[0] + short_net[1], axis=1, keepdims=True)
             result = jnp.where(lane == face, long_sum, result)
@@ -383,7 +383,7 @@
     for copy in row_copies:
         copy.wait()
     steps = 3 * COLS // GROUP
-    gather(rows, table, lanes, kappa, 0, steps // 2)
+    gather(rows, table, lanes, kappa, 0, steps // 6)
     own.wait()
     await_all("face", middle, send_sem.at[0], recv_sem.at[0])
     exchange(
@@ -391,7 +391,7 @@
     )
     own = pltpu.make_async_copy(middle.at[:, elem], incoming.at[elem], sems.at[7])
     own.start()
-    gather(rows, table, lanes, kappa, steps // 2, steps)
+    gather(rows, table, lanes, kappa, steps // 6, steps)
     own.wait()
     await_all("elem", incoming, send_sem.at[1], recv_sem.at[1])
     got = incoming[...].reshape(COLS, 128)

time: 43.7 us -> 43.8 us (level)
  no operation moved by 1% of the time
where the time goes in v4:
time: 43.8 us; the launch traced here: 43.6 us
  Pallas kernels  42.9 us (98%)
  between operations  0.65 us (1%)
    pallas_call x1, Pallas kernels, on_device(): pl.pallas_call(column_kernel, out_shape=(jax.ShapeDtypeStruct((COLS // 2,...  40.9 us
    pallas_call x1, Pallas kernels, on_device(): pl.pallas_call(home_kernel, out_shape=(field, field), in_specs=[vector, v...  2.05 us

profile of v4, /device:TPU:1, one launch (start us, length us, event | category | flops | bytes accessed | tf_op | source)
XLA Modules:
  0.0 43.6 jit_solution(16368670944459289601)
XLA Ops:
  0.6 40.9 %shard_map.194 = (f32[128,1,128]{2,1,0:T(1,128)}, f32[1,256]{1,0:T(1,128)}) custom-call(s32[2]{0:T(128)} %lit.1, s32[256,128]{1,0:T(8,128)} %bitcast.11, f32[24,256]{1,0:T(8,128)} %amount.1, f32[24,256]{1,0:T(8,128)} %scatter.1, f32[24,256]{1,0:T(8,128)} %cloud_path.1, f32[24,256]{1,0:T(8,128)} %planck.1, f32[24,256]{1,0:T(8,128)} %thickness.1, ...), custom_call_target="tpu_custom_call" | custom-call | tf_op jit(solution)/shard_map/pallas_call | solution.py:483
  41.5 2.0 %shard_map.195 = (f32[24,256]{1,0:T(8,128)}, f32[24,256]{1,0:T(8,128)}) custom-call(f32[128,1,128]{2,1,0:T(1,128)} %get-tuple-element.4.returned, f32[1,256]{1,0:T(1,128)} %get-tuple-element.5.slot), custom_call_target="tpu_custom_call" | custom-call | tf_op jit(solution)/shard_map/pallas_call | solution.py:535
